TPU v7x, 32 devices: a whole 2x2x4 slice. The times are simulated.
32 devices in a mesh: expert: 8 (over z, y), shard: 4 (over x, core).
Axes of the slice: x: 2, y: 2, z: 4, core: 2. Of those that a mesh axis runs over, the one named last changes fastest.
Arguments:
- tokens: bfloat16 [8192, 768], P(('expert', 'shard')), may hold values from -6 to 6
- norm1_gain: float32 [768], replicated, may hold values from 0.5 to 1.5
- qkv_weight: bfloat16 [3, 768, 768], P(None, None, 'shard'), may hold values from -0.21875 to 0.21875
- out_weight: bfloat16 [768, 768], P('shard'), may hold values from -1.25 to 1.25
- bucket_position_bias: float32 [32, 12], P(None, 'shard'), may hold values from -4 to 4
- norm2_gain: float32 [768], replicated, may hold values from 0.5 to 1.5
- router_weight: float32 [768, 8], replicated, may hold values from -0.109375 to 0.109375
- expert_in: bfloat16 [8, 768, 3072], P('expert', None, 'shard'), may hold values from -0.3125 to 0.3125
- expert_out: bfloat16 [8, 3072, 768], P('expert', 'shard'), may hold values from -0.875 to 0.875
- segment: int32 [8192], P('expert'), may hold values from 0 to 258, as said below
- route: int32 [8192], P(('expert', 'shard')), may hold values from 0 to 7
- slot: int32 [8192], P(('expert', 'shard')), may hold values from -1 to 39, as said below
- cotangent: bfloat16 [8192, 768], P(('expert', 'shard')), may hold values from -6 to 6
Outputs:
- output: bfloat16 [8192, 768], P(('expert', 'shard'))
- tokens_grad: float32 [8192, 768], P(('expert', 'shard'))
- norm1_gain_grad: float32 [768], replicated
- qkv_weight_grad: float32 [3, 768, 768], P(None, None, 'shard')
- output_weight_gradient: float32 [768, 768], P('shard')
- position_bias_grad: float32 [32, 12], P(None, 'shard')
- norm2_gain_grad: float32 [768], replicated
- router_weight_grad: float32 [768, 8], replicated
- expert_in_grad: float32 [8, 768, 3072], P('expert', None, 'shard')
- expert_out_grad: float32 [8, 3072, 768], P('expert', 'shard')
Inputs may be any that keep to these rules, and one draw needn't show every extreme that they name: `segment`: segment numbers never fall along a sequence of 1024 tokens; only equality within one sequence has meaning. slot is the token's rank, in order of position, among the tokens of its block of 256 with the same route, or -1 where that rank is 40 or more.
All inputs are finite; a program needn't handle non-finite values.
Results may differ from a plain program's by a relative error of at most 0.015.
Values may be sent and summed in bfloat16 or wider, within the bound.
No kernel may reach another device: no remote copies, remote signals or barrier semaphores. Data moves between devices by JAX's collectives and lax.ppermute only.
A program may use at most 128 MiB of HBM per device.

v0:
```python
import jax
import jax.numpy as jnp
from jax import lax
from jax.sharding import PartitionSpec as P

D = 768
HEAD_DIM = 64
BUCKETS = 32


EPS = 1e-06
THRESHOLDS = (12, 16, 23, 32, 46, 64, 91)


def bucket_of(relative):
    distance = jnp.abs(relative)
    far = 8 + sum(((distance >= edge).astype(jnp.int32) for edge in THRESHOLDS))
    near = jnp.where(distance < 8, distance, jnp.minimum(far, 15))
    return near + jnp.where(relative > 0, 16, 0)


def rms_norm(values, gain):
    return values * lax.rsqrt(jnp.mean(values * values, axis=-1, keepdims=True) + EPS) * gain


def gelu_tanh(values):
    return jax.nn.gelu(values, approximate=True)


def lift(rows, weight):
    return jnp.einsum("secd,edf->secf", rows, weight, preferred_element_type=jnp.float32)


def lower(active, weight):
    return jnp.einsum("secf,efd->secd", active, weight, preferred_element_type=jnp.float32)


def shards(
    tokens,
    norm1_gain,
    qkv_weight,
    out_weight,
    bucket_position_bias,
    norm2_gain,
    router_weight,
    expert_in,
    expert_out,
    segment,
    route,
    slot,
    cotangent,
):
    highest_precision = lax.Precision.HIGHEST
    tok_rows = tokens.shape[0]
    seq_rows = segment.shape[0]
    experts = router_weight.shape[1]
    capacity = (5 * tok_rows + 4 * experts - 1) // (4 * experts)
    local_heads = bucket_position_bias.shape[1]
    local_width = out_weight.shape[0]
    inputs = tokens.astype(jnp.float32)
    normed, norm1_back = jax.vjp(rms_norm, inputs, norm1_gain)
    normed_low = normed.astype(jnp.bfloat16)
    gathered = lax.all_gather(normed_low, "shard", axis=0, tiled=True)
    projected = jnp.einsum(
        "td,jde->jte", gathered, qkv_weight, preferred_element_type=jnp.float32
    ).astype(jnp.bfloat16)
    queries = projected[0].reshape(seq_rows, local_heads, HEAD_DIM)
    keys = projected[1].reshape(seq_rows, local_heads, HEAD_DIM)
    values = projected[2].reshape(seq_rows, local_heads, HEAD_DIM)
    block = min(512, seq_rows)
    block_count = seq_rows // block
    position = jnp.arange(seq_rows, dtype=jnp.int32)
    bucket_ids = jnp.arange(BUCKETS, dtype=jnp.int32)

    def block_scores(start):
        rows_query = lax.dynamic_slice_in_dim(queries, start, block, 0)
        row_position = lax.dynamic_slice_in_dim(position, start, block, 0)
        row_segment = lax.dynamic_slice_in_dim(segment, start, block, 0)
        bucket = bucket_of(position[None, :] - row_position[:, None])
        expert_indicator = (bucket[None, :, :] == bucket_ids[:, None, None]).astype(jnp.float32)
        bias_terms = jnp.einsum(
            "wut,wd->dut", expert_indicator, bucket_position_bias, precision=highest_precision
        )
        scores = (
            jnp.einsum("qhd,khd->hqk", rows_query, keys, preferred_element_type=jnp.float32) * 0.125
            + bias_terms
        )
        allowed = (row_segment[:, None] == segment[None, :])[None]
        return (jnp.where(allowed, scores, -1000000000.0), expert_indicator, rows_query)

    def forward_block(block_index):
        scores, expert_indicator, rows_query = block_scores(block_index * block)
        total = jax.nn.logsumexp(scores, axis=-1, keepdims=True)
        probs_low = jnp.exp(scores - total).astype(jnp.bfloat16)
        mixed = jnp.einsum("hqk,khd->qhd", probs_low, values, preferred_element_type=jnp.float32)
        return (mixed, total)

    mixed_blocks, totals = lax.map(forward_block, jnp.arange(block_count))
    mixed_low = mixed_blocks.reshape(seq_rows, local_width).astype(jnp.bfloat16)
    attended = lax.psum_scatter(
        jnp.dot(mixed_low, out_weight, preferred_element_type=jnp.float32),
        "shard",
        scatter_dimension=0,
        tiled=True,
    )
    hidden = inputs + attended
    routed, norm2_back = jax.vjp(rms_norm, hidden, norm2_gain)
    routed_low = routed.astype(jnp.bfloat16)
    chosen = (route[:, None] == jnp.arange(experts, dtype=jnp.int32)[None, :]).astype(jnp.float32)

    def gating(rows, weight):
        router_probs = jax.nn.softmax(jnp.dot(rows, weight, precision=highest_precision), axis=-1)
        return jnp.sum(router_probs * chosen, axis=-1)

    gate, gate_back = jax.vjp(gating, routed_low.astype(jnp.float32), router_weight)
    columns = jnp.arange(experts * capacity, dtype=jnp.int32)
    placed = ((route * capacity + slot)[:, None] == columns[None, :]) & (slot[:, None] >= 0)
    dispatch_low = placed.astype(jnp.bfloat16)
    dispatch_full = placed.astype(jnp.float32)
    outgoing = jnp.dot(dispatch_low.T, routed_low, preferred_element_type=jnp.float32).astype(
        jnp.bfloat16
    )
    arrived = lax.all_to_all(
        outgoing.reshape(experts, capacity, D), "expert", split_axis=0, concat_axis=0, tiled=True
    )
    sources = lax.axis_size("expert")
    arrived = arrived.reshape(sources, experts // sources, capacity, D)
    full_in, full_out = (
        lax.all_gather(expert_in, "shard", axis=2, tiled=True),
        lax.all_gather(expert_out, "shard", axis=1, tiled=True),
    )
    upward = lift(arrived, full_in)
    active, gelu_back = jax.vjp(gelu_tanh, upward)
    active_low = active.astype(jnp.bfloat16)
    produced = lower(active_low, full_out)
    returned = lax.all_to_all(
        produced.astype(jnp.bfloat16).reshape(experts, capacity, D),
        "expert",
        split_axis=0,
        concat_axis=0,
        tiled=True,
    )
    combined = jnp.dot(
        dispatch_low, returned.reshape(experts * capacity, D), preferred_element_type=jnp.float32
    )
    output = (hidden + gate[:, None] * combined).astype(jnp.bfloat16)
    upstream = cotangent.astype(jnp.float32)
    gate_grad = jnp.sum(upstream * combined, axis=-1)
    slot_grad = jnp.dot(
        dispatch_full.T, gate[:, None] * upstream, precision=highest_precision
    ).astype(jnp.bfloat16)
    owner_grad = lax.all_to_all(
        slot_grad.reshape(experts, capacity, D), "expert", split_axis=0, concat_axis=0, tiled=True
    )
    owner_grad = owner_grad.reshape(sources, experts // sources, capacity, D)
    active_grad = jnp.einsum(
        "secd,efd->secf", owner_grad, full_out, preferred_element_type=jnp.float32
    )
    upward_grad = gelu_back(active_grad)[0].astype(jnp.bfloat16)
    full_out_grad = jnp.einsum(
        "secf,secd->efd", active_low, owner_grad, preferred_element_type=jnp.float32
    )
    full_in_grad = jnp.einsum(
        "secd,secf->edf", arrived, upward_grad, preferred_element_type=jnp.float32
    )
    expert_in_grad, expert_out_grad = (
        lax.psum_scatter(
            full_in_grad.astype(jnp.bfloat16), "shard", scatter_dimension=2, tiled=True
        ).astype(jnp.float32),
        lax.psum_scatter(
            full_out_grad.astype(jnp.bfloat16), "shard", scatter_dimension=1, tiled=True
        ).astype(jnp.float32),
    )
    row_grad = jnp.einsum(
        "secf,edf->secd", upward_grad, full_in, preferred_element_type=jnp.float32
    )
    back_grad = lax.all_to_all(
        row_grad.reshape(experts, capacity, D).astype(jnp.bfloat16),
        "expert",
        split_axis=0,
        concat_axis=0,
        tiled=True,
    ).astype(jnp.float32)
    expert_grad = jnp.dot(
        dispatch_full, back_grad.reshape(experts * capacity, D), precision=highest_precision
    )
    router_rows_grad, router_grad = gate_back(gate_grad)
    hidden_part, norm2_grad = norm2_back(expert_grad + router_rows_grad)
    hidden_grad = upstream + hidden_part
    hidden_low = hidden_grad.astype(jnp.bfloat16)
    branch_grad = lax.all_gather(hidden_low, "shard", axis=0, tiled=True)
    mixed_grad = jnp.einsum(
        "td,ed->te", branch_grad, out_weight, preferred_element_type=jnp.float32
    ).astype(jnp.bfloat16)
    out_grad = jnp.einsum("te,td->ed", mixed_low, branch_grad, preferred_element_type=jnp.float32)
    mixed_grad = mixed_grad.reshape(seq_rows, local_heads, HEAD_DIM)

    def backward_block(carry, block_index):
        key_grad, value_grad, table_grad = carry
        start = block_index * block
        scores, expert_indicator, rows_query = block_scores(start)
        probs = jnp.exp(scores - totals[block_index])
        probs_low = probs.astype(jnp.bfloat16)
        rows_grad = lax.dynamic_slice_in_dim(mixed_grad, start, block, 0)
        prob_grad = jnp.einsum(
            "qhd,khd->hqk", rows_grad, values, preferred_element_type=jnp.float32
        )
        score_grad = probs * (prob_grad - jnp.sum(probs * prob_grad, axis=-1, keepdims=True))
        score_low = score_grad.astype(jnp.bfloat16)
        query_grad = (
            jnp.einsum("hqk,khd->qhd", score_low, keys, preferred_element_type=jnp.float32) * 0.125
        )
        key_grad = (
            key_grad
            + jnp.einsum("hqk,qhd->khd", score_low, rows_query, preferred_element_type=jnp.float32)
            * 0.125
        )
        value_grad = value_grad + jnp.einsum(
            "hqk,qhd->khd", probs_low, rows_grad, preferred_element_type=jnp.float32
        )
        rounded_scores = score_low.astype(jnp.float32)
        table_grad = table_grad + jnp.einsum(
            "fep,iep->if", rounded_scores, expert_indicator, precision=highest_precision
        )
        return ((key_grad, value_grad, table_grad), query_grad)

    zeros_heads = jnp.zeros((seq_rows, local_heads, HEAD_DIM), jnp.float32)
    initial = (zeros_heads, zeros_heads, jnp.zeros((BUCKETS, local_heads), jnp.float32))
    (key_grad, value_grad, table_grad), query_blocks = lax.scan(
        backward_block, initial, jnp.arange(block_count)
    )
    projected_grad = jnp.stack(
        [
            query_blocks.reshape(seq_rows, local_width),
            key_grad.reshape(seq_rows, local_width),
            value_grad.reshape(seq_rows, local_width),
        ]
    ).astype(jnp.bfloat16)
    qkv_grad = jnp.einsum(
        "td,jte->jde", gathered, projected_grad, preferred_element_type=jnp.float32
    )
    normed_grad = lax.psum_scatter(
        jnp.einsum(
            "jte,jde->td", projected_grad, qkv_weight, preferred_element_type=jnp.float32
        ).astype(jnp.bfloat16),
        "shard",
        scatter_dimension=0,
        tiled=True,
    ).astype(jnp.float32)
    input_part, norm1_grad = norm1_back(normed_grad)
    input_grad = hidden_grad + input_part
    qkv_grad, out_grad, table_grad = lax.psum((qkv_grad, out_grad, table_grad), "expert")
    norm1_grad, norm2_grad, router_grad = lax.psum(
        (norm1_grad, norm2_grad, router_grad), ("expert", "shard")
    )
    return (
        output,
        input_grad,
        norm1_grad,
        qkv_grad,
        out_grad,
        table_grad,
        norm2_grad,
        router_grad,
        expert_in_grad,
        expert_out_grad,
    )


def solution(mesh):
    placed = (
        P(("expert", "shard"), None),
        P(),
        P(None, None, "shard"),
        P("shard", None),
        P(None, "shard"),
        P(),
        P(),
        P("expert", None, "shard"),
        P("expert", "shard", None),
        P("expert"),
        P(("expert", "shard")),
        P(("expert", "shard")),
        P(("expert", "shard"), None),
    )
    return jax.shard_map(
        shards,
        mesh=mesh,
        in_specs=placed,
        out_specs=(
            P(("expert", "shard"), None),
            P(("expert", "shard"), None),
            P(),
            P(None, None, "shard"),
            P("shard", None),
            P(None, "shard"),
            P(),
            P(),
            P("expert", None, "shard"),
            P("expert", "shard", None),
        ),
        check_vma=False,
    )
```

profile of v0, /device:TPU:0, one launch (start us, length us, event | category | flops | bytes accessed | tf_op | source)
XLA Modules:
  0.0 713.5 jit_solution(12807872598505883635)
XLA Ops:
  11.6 22.4 %all-gather.5.cloned.1.call-done = bf16[1024,768]{1,0:T(8,128)(2,1)} async-done(((bf16[256,768]{1,0:T(8,128)(2,1)}), bf16[1024,768]{1,0:T(8,128)(2,1)}) %all-gather.5.cloned.1.call-update) | async-done | bytes 1572880 | tf_op jit(solution)/shard_map/all_gather | solution.py:63
  37.8 68.2 %while.32 = (s32[]{:T(128)}, bf16[2,512,3,64]{1,3,2,0:T(8,128)(2,1)S(1)}, f32[2,3,512,1]{2,1,3,0:T(4,128)S(1)}, s32[2]{0:T(128)S(1)}, s32[1024]{0:T(1024)S(1)}, ...) while((s32[]{:T(128)}, ...), condition=%wide.region_4.5_spmd.clone.clone, body=%wide.region_1.4_spmd.clone.clone.sunk | while | flops 1051734016 | bytes 38179420 | solution.py:98
  41.8 20.5 %fusion.215 = f32[512,1024,3]{1,2,0:T(4,128)S(1)} fusion(s32[512,1024]{1,0:T(8,128)S(1)} %fusion.214, f32[32,3]{0,1:T(4,128)S(1)} %get-tuple-element.554), kind=kOutput, calls=%fused_computation.3.clone.1 | convolution fusion | flops 620756992 | bytes 8388992 | tf_op jit(solution)/shard_map/while/body/eval_jaxpr/wut,wd->dut/dot_general | solution.py:81
  75.8 20.5 %fusion.215 = f32[512,1024,3]{1,2,0:T(4,128)S(1)} fusion(s32[512,1024]{1,0:T(8,128)S(1)} %fusion.214, f32[32,3]{0,1:T(4,128)S(1)} %get-tuple-element.554), kind=kOutput, calls=%fused_computation.3.clone.1 | convolution fusion | flops 620756992 | bytes 8388992 | tf_op jit(solution)/shard_map/while/body/eval_jaxpr/wut,wd->dut/dot_general | solution.py:81
  110.9 36.8 %reduce-scatter.5.cloned.1.call-done = f32[256,768]{1,0:T(8,128)} async-done(((f32[1024,768]{1,0:T(8,128)}), f32[256,768]{1,0:T(8,128)}) %reduce-scatter.5.cloned.1.call-update) | async-done | bytes 786448 | tf_op jit(solution)/shard_map/reduce_scatter | solution.py:100
  155.9 30.9 %all-gather.7.cloned.1.call-done = bf16[1,768,3072]{2,1,0:T(8,128)(2,1)} async-done(((bf16[1,768,768]{2,1,0:T(8,128)(2,1)}), bf16[1,768,3072]{2,1,0:T(8,128)(2,1)}) %all-gather.7.cloned.1.call-update) | async-done | bytes 4718608 | tf_op jit(solution)/shard_map/all_gather | solution.py:129
  193.6 32.2 %all-gather.9.cloned.1.call-done = bf16[1,3072,768]{2,1,0:T(8,128)(2,1)} async-done(((bf16[1,768,768]{2,1,0:T(8,128)(2,1)}), bf16[1,3072,768]{2,1,0:T(8,128)(2,1)}) %all-gather.9.cloned.1.call-update) | async-done | bytes 4718608 | tf_op jit(solution)/shard_map/all_gather | solution.py:130
  238.7 13.6 %all-to-all-done.1 = bf16[8,40,768]{2,1,0:T(8,128)(2,1)S(1)} async-done(((bf16[8,40,768]{2,1,0:T(8,128)(2,1)}), bf16[8,40,768]{2,1,0:T(8,128)(2,1)S(1)}, u32[]{:S(2)}, u32[]{:S(2)}) %all-to-all-start.1) | async-done | bytes 491552 | tf_op jit(solution)/shard_map/all_to_all | solution.py:136
  254.5 17.7 %all_to_all.20 = bf16[8,40,768]{2,1,0:T(8,128)(2,1)S(1)} all-to-all(bf16[8,40,768]{2,1,0:T(8,128)(2,1)S(1)} %bitcast.221), channel_id=1, replica_groups=mesh['expert'=8,'shard'=4] {'expert'}, dimensions={0} | all-to-all | bytes 983040 | tf_op jit(solution)/shard_map/all_to_all | solution.py:152
  272.2 7.4 %fusion.94 = bf16[8,40,3072]{2,1,0:T(8,128)(2,1)S(1)} fusion(f32[8,1,40,3072]{3,2,0,1:T(8,128)} %fusion.79, bf16[8,40,768]{2,1,0:T(8,128)(2,1)S(1)} %all_to_all.20, bf16[1,3072,768]{2,1,0:T(8,128)(2,1)} %all-gather.9.cloned.1.call-done), kind=kOutput, calls=%fused_computation.106 | convolution fusion | flops 1529610240 | bytes 11108352 | tf_op jit(solution)/shard_map/secd,efd->secf/dot_general | solution.py:156
  287.2 13.5 %all-to-all-done.3 = bf16[8,40,768]{2,1,0:T(8,128)(2,1)S(1)} async-done(((bf16[8,40,768]{2,1,0:T(8,128)(2,1)}), bf16[8,40,768]{2,1,0:T(8,128)(2,1)S(1)}, u32[]{:S(2)}, u32[]{:S(2)}) %all-to-all-start.3) | async-done | bytes 491552 | tf_op jit(solution)/shard_map/all_to_all | solution.py:177
  304.8 17.8 %all-gather.11.cloned.1.call-done = bf16[1024,768]{1,0:T(8,128)(2,1)} async-done(((bf16[256,768]{1,0:T(8,128)(2,1)}), bf16[1024,768]{1,0:T(8,128)(2,1)}) %all-gather.11.cloned.1.call-update) | async-done | bytes 1572880 | tf_op jit(solution)/shard_map/all_gather | solution.py:191
  326.3 127.0 %while.33 = (s32[]{:T(128)}, f32[1024,3,64]{0,2,1:T(8,128)}, f32[1024,3,64]{0,2,1:T(8,128)}, f32[32,3]{0,1:T(4,128)S(1)}, bf16[2,512,3,64]{1,3,2,0:T(8,128)(2,1)...) while((s32[]{:T(128)}, f32[1024,3,64]{0,2,1:T(8,128)}, ...), condition=%wide.region_15.16_spmd.clone.clone, body=%wide.region_13.15_spmd.clone.clone.sunk | while | flops 1777367808 | bytes 101502568 | solution.py:229
  347.6 21.9 %fusion.233 = f32[512,1024,3]{1,2,0:T(4,128)} fusion(s32[512,1024]{1,0:T(8,128)S(1)} %fusion.232, f32[32,3]{0,1:T(4,128)S(1)} %get-tuple-element.608), kind=kOutput, calls=%fused_computation.36.clone.1 | convolution fusion | flops 620756992 | bytes 8388992 | tf_op jit(solution)/shard_map/while/body/eval_jaxpr/wut,wd->dut/dot_general | solution.py:81
  369.4 7.5 %multiply_reduce_fusion.5 = (f32[3,512]{1,0:T(4,128)S(1)}, f32[3,512,1024]{2,1,0:T(8,128)S(1)}) fusion(f32[3,512,1024]{2,1,0:T(8,128)S(1)} %fusion.231, f32[3,512]{1,0:T(4,128)S(1)} %dynamic-slice_bitcast_fusion.2, f32[512,1024,3]{1,2,0:T(4,128)} %fusion.233, bf16[1024,3,64]{0,2,1:T(8,128)(2,1)S(1)} %get-tuple-element.606, ...), kind=kOutput, calls=%fused_computation.44.clone.1 | convolution fusion | flops 210762240 | bytes 22097924 | tf_op jit(solution)/shard_map/while/body/eval_jaxpr/qhd,khd->hqk/dot_general | solution.py:85
  381.2 11.3 %fusion.236 = f32[32,3]{0,1:T(4,128)S(1)} fusion(bf16[3,512,1024]{2,1,0:T(8,128)(2,1)S(1)} %copy-done.1, s32[512,1024]{1,0:T(8,128)S(1)} %fusion.232, f32[32,3]{0,1:T(4,128)S(1)} %get-tuple-element.582, pred[]{:T(512)S(6)} %compare.3), kind=kOutput, calls=%fused_computation.68.clone.1 | convolution fusion | flops 117440704 | bytes 5243649 | tf_op jit(solution)/shard_map/while/body/eval_jaxpr/fep,iep->if/dot_general | solution.py:222
  404.2 21.9 %fusion.233 = f32[512,1024,3]{1,2,0:T(4,128)} fusion(s32[512,1024]{1,0:T(8,128)S(1)} %fusion.232, f32[32,3]{0,1:T(4,128)S(1)} %get-tuple-element.608), kind=kOutput, calls=%fused_computation.36.clone.1 | convolution fusion | flops 620756992 | bytes 8388992 | tf_op jit(solution)/shard_map/while/body/eval_jaxpr/wut,wd->dut/dot_general | solution.py:81
  426.0 7.5 %multiply_reduce_fusion.5 = (f32[3,512]{1,0:T(4,128)S(1)}, f32[3,512,1024]{2,1,0:T(8,128)S(1)}) fusion(f32[3,512,1024]{2,1,0:T(8,128)S(1)} %fusion.231, f32[3,512]{1,0:T(4,128)S(1)} %dynamic-slice_bitcast_fusion.2, f32[512,1024,3]{1,2,0:T(4,128)} %fusion.233, bf16[1024,3,64]{0,2,1:T(8,128)(2,1)S(1)} %get-tuple-element.606, ...), kind=kOutput, calls=%fused_computation.44.clone.1 | convolution fusion | flops 210762240 | bytes 22097924 | tf_op jit(solution)/shard_map/while/body/eval_jaxpr/qhd,khd->hqk/dot_general | solution.py:85
  437.8 11.3 %fusion.236 = f32[32,3]{0,1:T(4,128)S(1)} fusion(bf16[3,512,1024]{2,1,0:T(8,128)(2,1)S(1)} %copy-done.1, s32[512,1024]{1,0:T(8,128)S(1)} %fusion.232, f32[32,3]{0,1:T(4,128)S(1)} %get-tuple-element.582, pred[]{:T(512)S(6)} %compare.3), kind=kOutput, calls=%fused_computation.68.clone.1 | convolution fusion | flops 117440704 | bytes 5243649 | tf_op jit(solution)/shard_map/while/body/eval_jaxpr/fep,iep->if/dot_general | solution.py:222
  460.0 7.2 %fusion.78 = bf16[1,3072,768]{2,1,0:T(8,128)(2,1)} fusion(bf16[8,40,768]{2,1,0:T(8,128)(2,1)S(1)} %copy-done.25, f32[8,1,40,3072]{3,2,0,1:T(8,128)} %fusion.79), kind=kOutput, calls=%fused_computation.94 | convolution fusion | flops 1521156096 | bytes 9142272 | tf_op jit(solution)/shard_map/secf,secd->efd/dot_general | solution.py:160
  481.0 22.2 %psum.45 = f32[32,3]{0,1:T(4,128)} all-reduce(f32[32,3]{0,1:T(4,128)S(1)} %get-tuple-element.159), channel_id=1, replica_groups=mesh['expert'=8,'shard'=4] {'expert'}, use_global_device_ids=true, to_apply=%region_22.23 | all-reduce | flops 96 | bytes 768 | tf_op jit(solution)/shard_map/psum | solution.py:252
  504.6 38.2 %all-reduce = (f32[768]{0:T(1024)}, f32[768]{0:T(1024)}, f32[768,8]{0,1:T(8,128)}) all-reduce(f32[768]{0:T(1024)S(1)} %get-tuple-element.291, f32[768]{0:T(1024)S(1)} %copy-done.49, f32[768,8]{0,1:T(8,128)S(1)} %fusion.145), channel_id=1, replica_groups=mesh['expert'=8,'shard'=4] {'expert','shard'}, use_global_device_ids=true, to_apply=%region_19.20 | all-reduce | flops 7680 | bytes 61440 | tf_op jit(solution)/shard_map/psum | solution.py:253
  548.6 41.1 %reduce-scatter.9.cloned.1.call-done = bf16[1,768,768]{2,1,0:T(8,128)(2,1)} async-done(((bf16[1,768,3072]{2,1,0:T(8,128)(2,1)}), bf16[1,768,768]{2,1,0:T(8,128)(2,1)}) %reduce-scatter.9.cloned.1.call-update) | async-done | bytes 1179664 | tf_op jit(solution)/shard_map/reduce_scatter | solution.py:167
  592.5 110.4 %all-reduce.4.cloned.1.call-done = (f32[3,768,192]{1,2,0:T(8,128)}, f32[192,768]{1,0:T(8,128)}) async-done(((f32[3,768,192]{1,2,0:T(8,128)}, f32[192,768]{1,0:T(8,128)}), (f32[3,768,192]{1,2,0:T(8,128)}, f32[192,768]{1,0:T(8,128)})) %all-reduce.4.cloned.1.call-update) | async-done | bytes 2359312 | tf_op jit(solution)/shard_map/psum | solution.py:252
  (265 shorter events, 144.5 us)
Async XLA Ops:
  7.2 26.8 %all-gather.5.cloned.1.call-start = ((), (), s32[]{:S(2)}) async-start(), calls=%async_computation.8 | async-start | bytes 1966080 | tf_op jit(solution)/shard_map/all_gather | solution.py:63
  11.5 136.2 %reduce-scatter.5.cloned.1.call-start = ((), (), s32[]{:S(2)}) async-start(), calls=%async_computation.9 | async-start | bytes 3932160 | tf_op jit(solution)/shard_map/reduce_scatter | solution.py:100
  37.8 69.4 %copy-start.29 = (bf16[192,768]{1,0:T(8,128)(2,1)S(1)}, bf16[192,768]{1,0:T(8,128)(2,1)}, u32[]{:S(2)}) copy-start(bf16[192,768]{1,0:T(8,128)(2,1)} %param.20) | copy-start | bytes 884740
  109.5 77.3 %all-gather.7.cloned.1.call-start = ((), (), s32[]{:S(2)}) async-start(), calls=%async_computation.10 | async-start | bytes 5898240 | tf_op jit(solution)/shard_map/all_gather | solution.py:129
  110.3 115.5 %all-gather.9.cloned.1.call-start = ((), (), s32[]{:S(2)}) async-start(), calls=%async_computation.11 | async-start | bytes 5898240 | tf_op jit(solution)/shard_map/all_gather | solution.py:130
  149.0 153.9 %copy-start.5 = (f32[256,768]{1,0:T(8,128)}, f32[256,768]{1,0:T(8,128)S(1)}, u32[]{:S(2)}) copy-start(f32[256,768]{1,0:T(8,128)S(1)} %get-tuple-element.349) | copy-start | bytes 2359300
  149.0 153.9 %copy-start.41 = (f32[256]{0:T(256)}, f32[256]{0:T(256)S(1)}, u32[]{:S(2)}) copy-start(f32[256]{0:T(256)S(1)} %fusion.142) | copy-start | bytes 3076
  149.2 89.0 %copy-start.12 = (bf16[256,768]{1,0:T(8,128)(2,1)}, bf16[256,768]{1,0:T(8,128)(2,1)S(1)}, u32[]{:S(2)}) copy-start(bf16[256,768]{1,0:T(8,128)(2,1)S(1)} %multiply_convert_fusion.2) | copy-start | bytes 1179652
  150.4 36.4 %all-to-all-start = ((bf16[8,40,768]{2,1,0:T(8,128)(2,1)}), bf16[8,40,768]{2,1,0:T(8,128)(2,1)S(1)}, u32[]{:S(2)}, u32[]{:S(2)}) async-start(bf16[8,40,768]{2,1,0:T(8,128)(2,1)} %bitcast.7), calls=%async_computation.1 | async-start | bytes 983040 | tf_op jit(solution)/shard_map/all_to_all | solution.py:123
  232.6 19.7 %all-to-all-start.1 = ((bf16[8,40,768]{2,1,0:T(8,128)(2,1)}), bf16[8,40,768]{2,1,0:T(8,128)(2,1)S(1)}, u32[]{:S(2)}, u32[]{:S(2)}) async-start(bf16[8,40,768]{2,1,0:T(8,128)(2,1)} %fusion.107), calls=%async_computation.2 | async-start | bytes 983040 | tf_op jit(solution)/shard_map/all_to_all | solution.py:136
  238.6 62.5 %copy-start.31 = (f32[256,8]{0,1:T(8,128)}, f32[256,8]{0,1:T(8,128)S(1)}, u32[]{:S(2)}) copy-start(f32[256,8]{0,1:T(8,128)S(1)} %get-tuple-element.360) | copy-start | bytes 24580
  238.7 62.5 %copy-start.37 = (f32[256]{0:T(256)}, f32[256]{0:T(256)S(1)}, u32[]{:S(2)}) copy-start(f32[256]{0:T(256)S(1)} %get-tuple-element.359) | copy-start | bytes 3076
  238.7 62.4 %copy-start.39 = (f32[256]{0:T(256)}, f32[256]{0:T(256)S(1)}, u32[]{:S(2)}) copy-start(f32[256]{0:T(256)S(1)} %fusion.140) | copy-start | bytes 3076
  283.5 17.2 %all-to-all-start.3 = ((bf16[8,40,768]{2,1,0:T(8,128)(2,1)}), bf16[8,40,768]{2,1,0:T(8,128)(2,1)S(1)}, u32[]{:S(2)}, u32[]{:S(2)}) async-start(bf16[8,40,768]{2,1,0:T(8,128)(2,1)} %fusion.104), calls=%async_computation.4 | async-start | bytes 983040 | tf_op jit(solution)/shard_map/all_to_all | solution.py:177
  287.2 35.5 %all-gather.11.cloned.1.call-start = ((), (), s32[]{:S(2)}) async-start(), calls=%async_computation.12 | async-start | bytes 1966080 | tf_op jit(solution)/shard_map/all_gather | solution.py:191
  304.8 198.4 %reduce-scatter.7.cloned.1.call-start = ((), (), s32[]{:S(2)}) async-start(), calls=%async_computation.13 | async-start | bytes 1966080 | tf_op jit(solution)/shard_map/reduce_scatter | solution.py:242
  459.9 85.8 %reduce-scatter.11.cloned.1.call-start = ((), (), s32[]{:S(2)}) async-start(), calls=%async_computation.15 | async-start | bytes 5898240 | tf_op jit(solution)/shard_map/reduce_scatter | solution.py:170
  467.2 122.5 %reduce-scatter.9.cloned.1.call-start = ((), (), s32[]{:S(2)}) async-start(), calls=%async_computation.14 | async-start | bytes 5898240 | tf_op jit(solution)/shard_map/reduce_scatter | solution.py:167
  473.4 229.5 %all-reduce.4.cloned.1.call-start = ((), (), s32[]{:S(2)}) async-start(), calls=%async_computation.16 | async-start | bytes 4718592 | tf_op jit(solution)/shard_map/psum | solution.py:252
  480.6 62.2 %copy-start.11 = (f32[256,768]{1,0:T(8,128)S(1)}, f32[256,768]{1,0:T(8,128)}, u32[]{:S(2)}) copy-start(f32[256,768]{1,0:T(8,128)} %copy-done.10) | copy-start | bytes 2359300
  480.6 62.2 %copy-start.35 = (f32[768]{0:T(1024)S(1)}, f32[768]{0:T(1024)}, u32[]{:S(2)}) copy-start(f32[768]{0:T(1024)} %param.22) | copy-start | bytes 9220
  480.6 62.2 %copy-start.42 = (f32[256]{0:T(256)S(1)}, f32[256]{0:T(256)}, u32[]{:S(2)}) copy-start(f32[256]{0:T(256)} %copy-done.41) | copy-start | bytes 3076
  480.6 62.2 %copy-start.53 = (f32[256]{0:T(256)S(1)}, f32[256]{0:T(256)}, u32[]{:S(2)}) copy-start(f32[256]{0:T(256)} %copy-done.52) | copy-start | bytes 3076
  480.6 62.2 %copy-start.57 = (f32[256]{0:T(256)S(1)}, f32[256]{0:T(256)}, u32[]{:S(2)}) copy-start(f32[256]{0:T(256)} %copy-done.56) | copy-start | bytes 3076
  (58 other events, 744.6 us)
Sparse Core Ops, SparseCore 0:
  11.6 22.3 all-gather.4
  109.7 37.9 reduce-scatter.4
  149.3 37.4 all-gather.6
  188.3 37.4 all-gather.8
  304.9 17.7 all-gather.10
  460.0 28.1 reduce-scatter.6
  490.8 48.1 reduce-scatter.10
  541.7 47.9 reduce-scatter.8
  593.8 109.0 all-reduce.3
where the time goes:
time: 727 us; the launch traced here: 714 us
  waiting for transfers between devices  320 us (44%)
  matrix products  208 us (29%)
  blocking collectives  78.1 us (11%)
  other arithmetic  35.1 us (5%)
  local copies, waits for them, and re-layouts  22 us (3%)
  loops' own time  20.2 us (3%)
  starting transfers between devices  15 us (2%)
  between operations  15 us (2%)
    psum x1, waiting for transfers between devices, shards(): lax.psum((qkv_grad, out_grad, table_grad), 'expert')  110 us
    dot_general x4, matrix products, block_scores(): jnp.einsum('wut,wd->dut', expert_indicator, bucket_position_bias, precisi...  84.8 us
    reduce_scatter x1, waiting for transfers between devices, shards(): lax.psum_scatter(full_in_grad.astype(jnp.bfloat16), 'shard', scatter_dime...  41.1 us
    psum x1, blocking collectives, shards(): lax.psum((norm1_grad, norm2_grad, router_grad), ('expert', 'shard'))  38.2 us
    reduce_scatter x1, waiting for transfers between devices, shards(): lax.psum_scatter(jnp.dot(mixed_low, out_weight, preferred_element_type=jn...  36.8 us
    all_gather x1, waiting for transfers between devices, shards(): lax.all_gather(expert_out, 'shard', axis=1, tiled=True)  32.2 us
    all_gather x1, waiting for transfers between devices, shards(): lax.all_gather(expert_in, 'shard', axis=2, tiled=True)  30.9 us
    dot_general x4, matrix products, block_scores(): jnp.einsum('qhd,khd->hqk', rows_query, keys, preferred_element_type=jnp.f...  26.4 us
  transfers between devices with their start and end apart: 12, of which 9 were waited for; matrix products, arithmetic and copies ran while one was open for 5% of the time, Pallas kernels for 0%

commit v1 on v0

v1 whole, which is shorter than its diff:
```python
import functools

import jax
import jax.numpy as jnp
from jax import lax
from jax.experimental import pallas as pl
from jax.experimental.pallas import tpu as pltpu
from jax.sharding import PartitionSpec as P

D = 768
HEAD_DIM = 64
BUCKETS = 32


EPS = 1e-06
THRESHOLDS = (12, 16, 23, 32, 46, 64, 91)
NEG = -1000000000.0
F32 = jnp.float32
BF16 = jnp.bfloat16


def bucket_of(relative):
    distance = jnp.abs(relative)
    far = 8 + sum(((distance >= edge).astype(jnp.int32) for edge in THRESHOLDS))
    near = jnp.where(distance < 8, distance, jnp.minimum(far, 15))
    return near + jnp.where(relative > 0, 16, 0)


def rms_norm(values, gain):
    return values * lax.rsqrt(jnp.mean(values * values, axis=-1, keepdims=True) + EPS) * gain


def gelu_tanh(values):
    return jax.nn.gelu(values, approximate=True)


def dot(a, b, ca=1, cb=0):
    return lax.dot_general(a, b, (((ca,), (cb,)), ((), ())), preferred_element_type=F32)


def swap(x, axis, bit):
    size = lax.axis_size(axis)
    return lax.ppermute(x, axis, [(i, i ^ bit) for i in range(size)])


def after(x, *others):
    return lax.optimization_barrier((x, *others))[0]


def exchange(rows, last=None):
    size = lax.axis_size("expert")
    count = rows.shape[0] // size
    if size != 8:
        return lax.all_to_all(rows, "expert", split_axis=0, concat_axis=0, tiled=True)
    blocks = [rows[k * count : (k + 1) * count] for k in range(size)]
    got = blocks[:1] + [swap(blocks[k], "expert", k) for k in range(1, 4)]
    if last is not None:
        blocks[4:] = lax.optimization_barrier((*blocks[4:], got[1], *last))[:4]
    return jnp.concatenate(got + [swap(blocks[k], "expert", k) for k in range(4, size)])


def build_bias(table_ref, head, tiles_ref, tok):
    wide = 4 * tok
    row = lax.broadcasted_iota(jnp.int32, (8, wide), 0)
    col = lax.broadcasted_iota(jnp.int32, (8, wide), 1)
    relative = col - tok - row - jnp.where(col >= 3 * tok, wide, 0)
    bucket = bucket_of(relative)
    base = jnp.zeros((8, wide), F32)
    for b in range(BUCKETS):
        base = jnp.where(bucket == b, table_ref[b, head], base)
    for a in range(tok // 8):
        rows = pltpu.roll(base, 8 * a, 1) if a else base
        for d in range(3):
            tiles_ref[d + 1, 8 * a : 8 * a + 8, :] = rows[:, d * tok : (d + 1) * tok]
    tiles_ref[0] = jnp.full((tok, tok), table_ref[15, head], F32)
    tiles_ref[4] = jnp.full((tok, tok), table_ref[31, head], F32)


def tile_index(me, j, l):
    return jnp.clip((me ^ l) - (me ^ j), -2, 2) + 2


def masked_scores(me, j, q, keys, tiles_ref, seg_col, seg_row_ref, blocks, tok):
    parts = []
    for l in range(blocks):
        s = dot(q, keys[l * tok : (l + 1) * tok], 1, 1)
        s = s + tiles_ref[tile_index(me, j, l)]
        parts.append(jnp.where(seg_col == seg_row_ref[me ^ l], s, NEG))
    return parts


def forward_kernel(
    me_ref, table_ref, seg_row_ref, seg_col_ref, x0, x1, x2a, x2b, x3a, x3b, w_ref,
    proj_ref, lse_ref, m0, m1, m2, m3, tiles_ref, mixed_ref,
):
    me = me_ref[0]
    heads = table_ref.shape[1]
    tok = x0.shape[0]
    half = tok // 2
    pieces = ((x0, 0), (x1, tok), (x2a, 2 * tok), (x2b, 2 * tok + half), (x3a, 3 * tok), (x3b, 3 * tok + half))
    for ref, start in pieces:
        rows = ref.shape[0]
        projected = dot(ref[...], w_ref[...], 1, 1).astype(BF16)
        for which in range(3):
            for h in range(heads):
                at = (3 * h + which) * HEAD_DIM
                part = projected[:, at : at + HEAD_DIM]
                if which == 0:
                    part = part * jnp.asarray(0.125, BF16)
                proj_ref[which, h, start : start + rows, :] = part
    for h in range(heads):
        build_bias(table_ref, h, tiles_ref, tok)

        def block(j, carry):
            q = proj_ref[0, h, pl.ds(pl.multiple_of(j * tok, tok), tok), :]
            keys = proj_ref[1, h]
            seg_col = seg_col_ref[me ^ j]
            parts = masked_scores(me, j, q, keys, tiles_ref, seg_col, seg_row_ref, 4, tok)
            top = functools.reduce(jnp.maximum, parts)
            top = jnp.max(top, axis=1, keepdims=True)
            probs = [jnp.exp(s - top) for s in parts]
            total = jnp.sum(functools.reduce(jnp.add, probs), axis=1, keepdims=True)
            mixed = None
            for l in range(4):
                term = dot(probs[l].astype(BF16), proj_ref[2, h, l * tok : (l + 1) * tok, :])
                mixed = term if mixed is None else mixed + term
            mixed_ref[h, pl.ds(pl.multiple_of(j * tok, tok), tok), :] = (mixed / total).astype(BF16)
            lse_ref[h, pl.ds(pl.multiple_of(j * tok, tok), tok), :] = jnp.broadcast_to(
                top + jnp.log(total), (tok, 128)
            )
            return carry

        lax.fori_loop(0, 4, block, 0)
    for j, out in enumerate((m0, m1, m2, m3)):
        out[...] = jnp.concatenate(
            [mixed_ref[h, j * tok : (j + 1) * tok, :] for h in range(heads)], axis=1
        )


def backward_kernel(
    h, final, me_ref, table_ref, seg_row_ref, seg_col_ref, x0, x1, x2a, x2b, x3a, x3b, w_ref, gain_ref,
    proj_ref, lse_ref, g0, g1, g2, g3, *rest,
):
    me = me_ref[0]
    heads = table_ref.shape[1]
    tok = x0.shape[0]
    half = tok // 2
    if h:
        earlier, extra_before, *rest = rest
    dp_before, rest = (rest[: h - 1], rest[h - 1 :]) if final else ((), rest)
    if final:
        normed_grad_ref, *rest = rest
    else:
        dp_out, *rest = rest
    payload_ref, extra_ref, tiles_ref, sums_ref, do_ref, dkt_ref, dvt_ref, dp_ref, dpt_ref = rest
    width = HEAD_DIM
    for j, ref in enumerate((g0, g1, g2, g3)):
        do_ref[j * tok : (j + 1) * tok, :] = ref[:, h * width : (h + 1) * width]
    build_bias(table_ref, h, tiles_ref, tok)
    sums_ref[...] = jnp.zeros_like(sums_ref)
    dkt_ref[...] = jnp.zeros_like(dkt_ref)
    dvt_ref[...] = jnp.zeros_like(dvt_ref)

    def block(j, carry):
        rows = pl.ds(pl.multiple_of(j * tok, tok), tok)
        q = proj_ref[0, 0, rows, :]
        grad = do_ref[rows, :]
        seg_col = seg_col_ref[me ^ j]
        parts = masked_scores(me, j, q, proj_ref[1, 0], tiles_ref, seg_col, seg_row_ref, 4, tok)
        lse = lse_ref[0, rows, :][:, :1]
        probs, weighted = [], []
        for l in range(4):
            p = jnp.exp(parts[l] - lse)
            cut = slice(l * tok, (l + 1) * tok)
            dvt_ref[:, cut] += dot(grad, p.astype(BF16), 0, 0)
            probs.append(p)
            weighted.append(p * dot(grad, proj_ref[2, 0, cut, :], 1, 1))
        delta = jnp.sum(functools.reduce(jnp.add, weighted), axis=1, keepdims=True)
        dq = None
        for l in range(4):
            cut = slice(l * tok, (l + 1) * tok)
            ds = weighted[l] - probs[l] * delta
            at = tile_index(me, j, l)
            sums_ref[at] = sums_ref[at] + ds
            low = ds.astype(BF16)
            dkt_ref[:, cut] += dot(q, low, 0, 0)
            term = dot(low, proj_ref[1, 0, cut, :])
            dq = term if dq is None else dq + term
        dq = dq * 0.125
        dp_ref[rows, :width] = dq.astype(BF16)
        dpt_ref[j, :width, :] = dq.T.astype(BF16)
        return carry

    lax.fori_loop(0, 4, block, 0)
    dkt = dkt_ref[...]
    dvt = dvt_ref[...]
    dp_ref[:, width : 2 * width] = dkt.T.astype(BF16)
    dp_ref[:, 2 * width :] = dvt.T.astype(BF16)
    for j in range(4):
        cut = slice(j * tok, (j + 1) * tok)
        dpt_ref[j, width : 2 * width, :] = dkt[:, cut].astype(BF16)
        dpt_ref[j, 2 * width :, :] = dvt[:, cut].astype(BF16)

    strip = jnp.concatenate([sums_ref[1], sums_ref[2], sums_ref[3], jnp.zeros((tok, tok), F32)], axis=1)
    rows = tok
    while rows > 8:
        rows //= 2
        strip = strip[:rows] + pltpu.roll(strip[rows:], 4 * tok - rows, 1)
    diagonal = strip[0:1]
    for i in range(1, 8):
        diagonal = diagonal + pltpu.roll(strip[i : i + 1], 4 * tok - i, 1)
    col = lax.broadcasted_iota(jnp.int32, (1, 4 * tok), 1)
    bucket = bucket_of(col - tok - jnp.where(col >= 3 * tok, 4 * tok, 0))
    low_far = jnp.sum(jnp.sum(sums_ref[0], axis=0, keepdims=True), axis=1, keepdims=True)
    high_far = jnp.sum(jnp.sum(sums_ref[4], axis=0, keepdims=True), axis=1, keepdims=True)
    lane = lax.broadcasted_iota(jnp.int32, (1, D), 1) - me * (BUCKETS * heads)
    table_row = jnp.zeros((1, D), F32)
    for b in range(BUCKETS):
        value = jnp.sum(jnp.where(bucket == b, diagonal, 0.0), axis=1, keepdims=True)
        if b == 15:
            value = value + low_far
        if b == 31:
            value = value + high_far
        table_row = jnp.where(lane == b * heads + h, value, table_row)

    pieces = ((x0, 0, 0), (x1, 1, 0), (x2a, 2, 0), (x2b, 2, half), (x3a, 3, 0), (x3b, 3, half))
    total = None
    for ref, j, start in pieces:
        term = dot(dpt_ref[j, :, start : start + ref.shape[0]], ref[...])
        total = term if total is None else total + term
    payload_ref[...] = total.astype(BF16)
    gain_row = jnp.sum(total * w_ref[h].astype(F32), axis=0, keepdims=True) / gain_ref[...]
    row = lax.broadcasted_iota(jnp.int32, (8, D), 0)
    extra = jnp.where(row == 0, gain_row, jnp.where(row == 1, table_row, 0.0))
    extra_ref[...] = extra + extra_before[...] if h else extra
    if final:
        for j in range(4):
            cut = slice(j * tok, (j + 1) * tok)
            part = dot(dp_ref[cut, :], w_ref[h])
            for i, ref in enumerate((earlier, *dp_before)[: h]):
                part = part + dot(ref[cut, :], w_ref[i])
            normed_grad_ref[cut, :] = part.astype(BF16)
    else:
        dp_out[...] = dp_ref[...]


VMEM = pl.BlockSpec(memory_space=pltpu.VMEM)
SMEM = pl.BlockSpec(memory_space=pltpu.SMEM)
PARAMS = pltpu.CompilerParams(vmem_limit_bytes=48 * 1024 * 1024)


def halves(x, bit):
    n = x.shape[0] // 2
    upper = (lax.axis_index("expert") & bit) != 0
    keep = jnp.where(upper, x[n:], x[:n])
    send = jnp.where(upper, x[:n], x[n:])
    return keep, send


def add_low(a, b):
    return (a.astype(F32) + b.astype(F32)).astype(BF16)


def joined(x, other, bit):
    upper = (lax.axis_index("expert") & bit) != 0
    return jnp.concatenate([jnp.where(upper, other, x), jnp.where(upper, x, other)])


def shards(
    tokens,
    norm1_gain,
    qkv_weight,
    out_weight,
    bucket_position_bias,
    norm2_gain,
    router_weight,
    expert_in,
    expert_out,
    segment,
    route,
    slot,
    cotangent,
):
    highest_precision = lax.Precision.HIGHEST
    tok = tokens.shape[0]
    half = tok // 2
    seq = segment.shape[0]
    experts = router_weight.shape[1]
    capacity = (5 * tok + 4 * experts - 1) // (4 * experts)
    heads = bucket_position_bias.shape[1]
    width = out_weight.shape[0]
    me = lax.axis_index("shard").astype(jnp.int32).reshape(1)
    sources = lax.axis_size("expert")

    def over_x(v):
        return swap(v, "shard", 2)

    def over_core(v):
        return swap(v, "shard", 1)

    inputs = tokens.astype(F32)
    s1 = lax.rsqrt(jnp.mean(inputs * inputs, axis=-1, keepdims=True) + EPS)
    normed_low = (inputs * s1 * norm1_gain).astype(BF16)
    x2a = over_x(normed_low[:half])
    x2b = over_x(normed_low[half:])
    x1 = over_core(normed_low)
    x3a = over_core(x2a)
    x3b = over_core(x2b)
    pieces = (normed_low, x1, x2a, x2b, x3a, x3b)
    out_w1 = over_core(out_weight)
    out_w2 = over_x(after(out_weight, x2b))
    in_own, out_own = expert_in[0], expert_out[0]
    split_in, split_out = 5 * D // 8, D // 3
    in_far = over_x(in_own[:split_in])
    qkv_t = jnp.transpose(qkv_weight.reshape(3, D, heads, HEAD_DIM), (2, 0, 3, 1))
    qkv_t = qkv_t.reshape(heads, 3 * HEAD_DIM, D)
    seg_rows = segment.reshape(4, 1, tok)
    seg_cols = segment.reshape(4, tok, 1)

    sds = jax.ShapeDtypeStruct
    proj, lse, *mixed = pl.pallas_call(
        forward_kernel,
        out_shape=[sds((3, heads, seq, HEAD_DIM), BF16), sds((heads, seq, 128), F32)]
        + [sds((tok, width), BF16)] * 4,
        in_specs=[SMEM, SMEM] + [VMEM] * 9,
        out_specs=[VMEM] * 6,
        scratch_shapes=[pltpu.VMEM((5, tok, tok), F32), pltpu.VMEM((heads, seq, HEAD_DIM), BF16)],
        compiler_params=PARAMS,
        cost_estimate=pl.CostEstimate(flops=15 * 10**9, bytes_accessed=8 * 10**6, transcendentals=3 * 10**6),
        name="attention_forward",
    )(me, bucket_position_bias, seg_rows, seg_cols, *pieces, qkv_t.reshape(3 * width, D))

    *mixed, in_far, out_w2 = lax.optimization_barrier((*mixed, in_far, out_w2))
    out_w3 = over_core(out_w2)
    out_w = jnp.concatenate([out_weight, out_w1, out_w2, out_w3])
    in_rest = over_x(after(in_own[split_in:], in_far))
    out_far = over_x(after(out_own[:split_out], in_far))
    out_rest = over_x(after(out_own[split_out:], out_far))
    mixed_own = jnp.concatenate(
        [mixed[0]] + [swap(mixed[k], "shard", k) for k in (1, 2, 3)], axis=1
    )
    attended = dot(mixed_own, out_w)
    hidden = inputs + attended
    s2 = lax.rsqrt(jnp.mean(hidden * hidden, axis=-1, keepdims=True) + EPS)
    routed_low = (hidden * s2 * norm2_gain).astype(BF16)
    routed_full = routed_low.astype(F32)
    chosen = (route[:, None] == jnp.arange(experts, dtype=jnp.int32)[None, :]).astype(F32)
    router_probs = jax.nn.softmax(jnp.dot(routed_full, router_weight, precision=highest_precision), axis=-1)
    gate = jnp.sum(router_probs * chosen, axis=-1, keepdims=True)
    upstream = cotangent.astype(F32)

    columns = jnp.arange(experts * capacity, dtype=jnp.int32)
    if sources == 8:
        order = columns // capacity ^ (lax.axis_index("expert") * (experts // sources))
        columns = order * capacity + columns % capacity
    placed = ((route * capacity + slot)[:, None] == columns[None, :]) & (slot[:, None] >= 0)
    dispatch = placed.astype(BF16)
    both = jnp.concatenate([routed_low, (gate * upstream).astype(BF16)], axis=1)
    outgoing = dot(dispatch, both, 0, 0).astype(BF16)
    arrived = exchange(outgoing, (in_rest, out_far))
    arrived, out_rest = lax.optimization_barrier((arrived, out_rest))
    in_far = jnp.concatenate([in_far, in_rest])
    out_far = jnp.concatenate([out_far, out_rest])
    beside = over_core(arrived)
    rows = jnp.concatenate([arrived[:, :D], beside[:, :D]])
    grads = jnp.concatenate([arrived[:, D:], beside[:, D:]])
    count = experts * capacity

    def expert_half(w_in, w_out):
        upward = dot(rows, w_in)
        active, gelu_back = jax.vjp(gelu_tanh, upward)
        active = active.astype(BF16)
        active_grad = dot(grads, w_out, 1, 1)
        upward_grad = gelu_back(active_grad)[0].astype(BF16)
        return active, upward_grad

    active_far, upward_far = expert_half(in_far, out_far)
    in_grad_far = over_x(dot(rows, upward_far, 0, 0).astype(BF16))
    out_grad_far = dot(active_far, grads, 0, 0).astype(BF16)
    active_own, upward_own = expert_half(in_own, out_own)
    produced = dot(active_own, out_own) + dot(active_far, out_far)
    row_grad = dot(upward_own, in_own, 1, 1) + dot(upward_far, in_far, 1, 1)
    mine = jnp.concatenate([produced[:count], row_grad[:count]], axis=1)
    theirs = jnp.concatenate([produced[count:], row_grad[count:]], axis=1).astype(BF16)
    returned = exchange(add_low(mine, over_core(theirs)))
    returned, in_grad_far = lax.optimization_barrier((returned, in_grad_far))
    in_grad_own = dot(rows, upward_own, 0, 0)
    out_grad_own = dot(active_own, grads, 0, 0)
    back = dot(dispatch, returned)
    combined, expert_grad = back[:, :D], back[:, D:]
    output = (hidden + gate * combined).astype(BF16)
    gate_grad = jnp.sum(upstream * combined, axis=-1, keepdims=True)
    logit_grad = router_probs * (gate_grad * chosen - gate_grad * gate)
    router_grad = lax.dot_general(
        logit_grad, routed_full, (((0,), (0,)), ((), ())), precision=highest_precision
    )
    routed_grad = expert_grad + lax.dot_general(
        logit_grad, router_weight, (((1,), (1,)), ((), ())), precision=highest_precision
    )
    norm2_grad = jnp.sum(routed_grad * hidden * s2, axis=0, keepdims=True)
    scaled = routed_grad * norm2_gain
    hidden_grad = (
        upstream + s2 * scaled - hidden * s2**3 * jnp.mean(scaled * hidden, axis=-1, keepdims=True)
    )
    branch_low = hidden_grad.astype(BF16)
    mixed_grad = dot(branch_low, out_w, 1, 1).astype(BF16)
    mixed_grads = [mixed_grad[:, :width]] + [
        swap(mixed_grad[:, k * width : (k + 1) * width], "shard", k) for k in (1, 2, 3)
    ]
    branch1 = over_core(branch_low)
    branch2 = over_x(after(branch_low, mixed_grads[2], mixed_grads[3]))
    def head_gradients(h, grads, earlier):
        final = h == heads - 1
        one = pl.BlockSpec((3, 1, seq, HEAD_DIM), lambda i: (0, h, 0, 0))
        log = pl.BlockSpec((1, seq, 128), lambda i: (h, 0, 0))
        return pl.pallas_call(
            functools.partial(backward_kernel, h, final),
            grid=(1,),
            out_shape=[
                sds((seq, D), BF16) if final else sds((seq, 3 * HEAD_DIM), BF16),
                sds((3 * HEAD_DIM, D), BF16),
                sds((8, D), F32),
            ],
            in_specs=[SMEM, SMEM] + [VMEM] * 10 + [one, log] + [VMEM] * (4 + len(earlier)),
            out_specs=[VMEM] * 3,
            scratch_shapes=[
                pltpu.VMEM((5, tok, tok), F32),
                pltpu.VMEM((5, tok, tok), F32),
                pltpu.VMEM((seq, HEAD_DIM), BF16),
                pltpu.VMEM((HEAD_DIM, seq), F32),
                pltpu.VMEM((HEAD_DIM, seq), F32),
                pltpu.VMEM((seq, 3 * HEAD_DIM), BF16),
                pltpu.VMEM((4, 3 * HEAD_DIM, tok), BF16),
            ],
            compiler_params=PARAMS,
            cost_estimate=pl.CostEstimate(flops=8 * 10**9, bytes_accessed=6 * 10**6, transcendentals=10**6),
            name="attention_backward_%d" % h,
        )(
            me, bucket_position_bias, seg_rows, seg_cols, *pieces, qkv_t, norm1_gain.reshape(1, D),
            proj, lse, *grads, *earlier,
        )

    dps, payloads, extra = [], [], None
    for h in range(heads):
        if h == 1:
            mixed_grads[0], branch2 = lax.optimization_barrier((mixed_grads[0], branch2))
        earlier = []
        if h:
            earlier = [dps[0], extra]
        if h == heads - 1:
            earlier += dps[1:]
        dp, payload, extra = head_gradients(h, mixed_grads, earlier)
        dps.append(dp)
        payloads.append(payload)
    normed_part = dps[-1]
    branch3 = over_core(branch2)
    out_grad = sum(dot(mixed[k], b, 0, 0) for k, b in enumerate((branch_low, branch1, branch2, branch3)))
    small = jnp.concatenate([norm2_grad, router_grad])
    small = jnp.concatenate([small, extra[:2]])
    wide = [
        jnp.concatenate(payloads[1:]),
        jnp.concatenate([payloads[0], out_grad.astype(BF16)]),
    ]
    in_step = sources == 8
    bits = ((1, 2), (2, 1))
    pair = normed_part.reshape(2, 2, tok, D)
    small_other, normed_other = over_core(small), over_core(pair[:, 1])
    out_grad_far = over_x(after(out_grad_far, branch2))
    if in_step:
        cuts = [halves(part, bit[0]) for part, bit in zip(wide, bits)]
        got = [swap(send, "expert", bit[0]) for (_, send), bit in zip(cuts, bits)]
        *got, small_other, normed_other, out_grad_far = lax.optimization_barrier(
            (*got, small_other, normed_other, out_grad_far)
        )
        wide = [add_low(keep, other) for (keep, _), other in zip(cuts, got)]
    small = small + small_other
    near = pair[:, 0].astype(F32) + normed_other.astype(F32)
    small_other, normed_other = over_x(small), over_x(near[1].astype(BF16))
    expert_in_grad = (in_grad_own + in_grad_far.astype(F32))[None]
    if in_step:
        cuts = [halves(part, bit[1]) for part, bit in zip(wide, bits)]
        got = [swap(send, "expert", bit[1]) for (_, send), bit in zip(cuts, bits)]
        *got, small_other, normed_other, expert_in_grad = lax.optimization_barrier(
            (*got, small_other, normed_other, expert_in_grad)
        )
        wide = [add_low(keep, other) for (keep, _), other in zip(cuts, got)]
    small = small + small_other
    normed_grad = near[0] + normed_other.astype(F32)
    scaled1 = normed_grad * norm1_gain
    input_grad = (
        hidden_grad
        + s1 * scaled1
        - inputs * s1**3 * jnp.mean(scaled1 * inputs, axis=-1, keepdims=True)
    )
    expert_out_grad = (out_grad_own + out_grad_far.astype(F32))[None]
    if in_step:
        got = [swap(part, "expert", 4) for part in wide]
        small_other = swap(small, "expert", 1)
        *got, small_other, input_grad, expert_out_grad = lax.optimization_barrier(
            (*got, small_other, input_grad, expert_out_grad)
        )
        wide = [add_low(part, other) for part, other in zip(wide, got)]
        small = small + small_other
        for step, bit_small in ((1, 2), (0, 4)):
            got = [swap(part, "expert", bit[step]) for part, bit in zip(wide, bits)]
            small_other = swap(small, "expert", bit_small)
            *got, small_other = lax.optimization_barrier((*got, small_other))
            wide = [joined(part, other, bit[step]) for part, other, bit in zip(wide, got, bits)]
            small = small + small_other
        one, two = wide
    else:
        one, two, small = lax.psum((wide[0].astype(F32), wide[1].astype(F32), small), "expert")
    qkv_grad = jnp.concatenate([two[: 3 * HEAD_DIM], one])
    qkv_grad = jnp.transpose(qkv_grad.reshape(heads, 3, HEAD_DIM, D), (1, 3, 0, 2))
    qkv_grad = qkv_grad.reshape(3, D, width).astype(F32)
    norm1_grad = small[experts + 1]
    table_size = BUCKETS * heads
    table_grad = lax.dynamic_slice_in_dim(small[experts + 2], me[0] * table_size, table_size)
    table_grad = table_grad.reshape(BUCKETS, heads)
    return (
        output,
        input_grad,
        norm1_grad,
        qkv_grad,
        two[3 * HEAD_DIM :].astype(F32),
        table_grad,
        small[0],
        jnp.transpose(small[1 : experts + 1]),
        expert_in_grad,
        expert_out_grad,
    )


def solution(mesh):
    placed = (
        P(("expert", "shard"), None),
        P(),
        P(None, None, "shard"),
        P("shard", None),
        P(None, "shard"),
        P(),
        P(),
        P("expert", None, "shard"),
        P("expert", "shard", None),
        P("expert"),
        P(("expert", "shard")),
        P(("expert", "shard")),
        P(("expert", "shard"), None),
    )
    return jax.shard_map(
        shards,
        mesh=mesh,
        in_specs=placed,
        out_specs=(
            P(("expert", "shard"), None),
            P(("expert", "shard"), None),
            P(),
            P(None, None, "shard"),
            P("shard", None),
            P(None, "shard"),
            P(),
            P(),
            P("expert", None, "shard"),
            P("expert", "shard", None),
        ),
        check_vma=False,
    )
```

time: 727 us -> 254 us (0.35); the launches traced: 714 us -> 249 us
  waiting for transfers between devices: 320 us -> 81.9 us
  matrix products: 208 us -> 23.1 us
  blocking collectives: 78.1 us -> 0 us
  starting transfers between devices: 15 us -> 69.6 us
  Pallas kernels: 0 us -> 39.5 us
  other arithmetic: 35.1 us -> 12.2 us
  loops' own time: 20.2 us -> 0 us
  between operations: 15 us -> 2.51 us
    dot_general x38 -> x23, matrix products: 206 us -> 23.1 us  [the longest x20 21.3 us: dot(): lax.dot_general(a, b, (((ca,), (cb,)), ((), ())), preferred_element_type=...]
    psum x1 -> x0, waiting for transfers between devices: 110 us -> none  [shards(): lax.psum((qkv_grad, out_grad, table_grad), 'expert')]
    all_gather x4 -> x0, waiting for transfers between devices: 103 us -> none  [the longest x1 32.2 us: shards(): lax.all_gather(expert_out, 'shard', axis=1, tiled=True)]
    ppermute x0 -> x56, waiting for transfers between devices: none -> 81.9 us  [swap(): return lax.ppermute(x, axis, [(i, i ^ bit) for i in range(size)])]
    reduce_scatter x4 -> x0, waiting for transfers between devices: 77.9 us -> none  [the longest x1 41.1 us: shards(): lax.psum_scatter(full_in_grad.astype(jnp.bfloat16), 'shard', scatter_dime...]
    ppermute x0 -> x56, starting transfers between devices: none -> 69.6 us  [swap(): return lax.ppermute(x, axis, [(i, i ^ bit) for i in range(size)])]
    psum x2 -> x0, blocking collectives: 60.4 us -> none  [the longest x1 38.2 us: shards(): lax.psum((norm1_grad, norm2_grad, router_grad), ('expert', 'shard'))]
    pallas_call x0 -> x4, Pallas kernels: none -> 39.5 us  [the longest x3 26 us: head_gradients(): pl.pallas_call(functools.partial(backward_kernel, h, final), grid=(1,), o...]
  transfers between devices with their start and end apart: 12 -> 56, of which waited for: 9 -> 20; matrix products, arithmetic and copies ran while one was open for 5% -> 9% of each run, Pallas kernels for 0% -> 16%
where the time goes in v1:
time: 254 us; the launch traced here: 249 us
  waiting for transfers between devices  81.9 us (32%)
  starting transfers between devices  69.6 us (27%)
  Pallas kernels  39.5 us (16%)
  matrix products  23.1 us (9%)
  local copies, waits for them, and re-layouts  20 us (8%)
  other arithmetic  12.2 us (5%)
    ppermute x56, waiting for transfers between devices, swap(): return lax.ppermute(x, axis, [(i, i ^ bit) for i in range(size)])  81.9 us
    ppermute x56, starting transfers between devices, swap(): return lax.ppermute(x, axis, [(i, i ^ bit) for i in range(size)])  69.6 us
    pallas_call x3, Pallas kernels, head_gradients(): pl.pallas_call(functools.partial(backward_kernel, h, final), grid=(1,), o...  26 us
    dot_general x20, matrix products, dot(): lax.dot_general(a, b, (((ca,), (cb,)), ((), ())), preferred_element_type=...  21.3 us
    pallas_call x1, Pallas kernels, shards(): pl.pallas_call(forward_kernel, out_shape=[sds((3, heads, seq, HEAD_DIM),...  13.5 us
    unnamed x157, local copies, waits for them, and re-layouts  11.4 us
  transfers between devices with their start and end apart: 56, of which 20 were waited for; matrix products, arithmetic and copies ran while one was open for 9% of the time, Pallas kernels for 16%

profile of v1, /device:TPU:0, one launch (start us, length us, event | category | flops | bytes accessed | tf_op | source)
XLA Modules:
  0.0 248.9 jit_solution(13565932071324711998)
XLA Ops:
  15.5 2.9 %collective-permute-done.1.x2a = bf16[128,768]{1,0:T(8,128)(2,1)S(1)} collective-permute-done((bf16[128,768]{1,0:T(8,128)(2,1)}, bf16[128,768]{1,0:T(8,128)(2,1)S(1)}, u32[]{:S(2)}, u32[]{:S(2)}) %collective-permute-start.1) | collective-permute-done | bytes 196640 | tf_op jit(solution)/shard_map/ppermute | solution.py:43
  20.4 13.5 %attention_forward.1 = (bf16[3,3,1024,64]{3,2,1,0:T(8,128)(2,1)}, f32[3,1024,128]{2,1,0:T(8,128)S(1)}, bf16[256,192]{1,0:T(8,128)(2,1)S(1)}, bf16[256,192]{1,0:T...) custom-call(s32[1]{0:T(128)} %bitcast.me_ref, f32[32,3]{1,0:T(8,128)S(1)} %copy.31.table_ref, ...), custom_call_target="tpu_custom_call" | custom-call | flops 15000000512 | bytes 8000000 | tf_op jit(solution)/shard_map/attention_forward/pallas_call | solution.py:321
  33.9 6.4 %collective-permute-done.6 = bf16[192,768]{1,0:T(8,128)(2,1)S(1)} collective-permute-done((bf16[192,768]{1,0:T(8,128)(2,1)}, bf16[192,768]{1,0:T(8,128)(2,1)S(1)}, u32[]{:S(2)}, u32[]{:S(2)}) %collective-permute-start.6) | collective-permute-done | bytes 294944 | tf_op jit(solution)/shard_map/ppermute | solution.py:43
  45.1 2.9 %collective-permute-done.8 = bf16[256,192]{1,0:T(8,128)(2,1)S(1)} collective-permute-done((bf16[256,192]{1,0:T(8,128)(2,1)S(1)}, bf16[256,192]{1,0:T(8,128)(2,1)S(1)}, u32[]{:S(2)}, u32[]{:S(2)}) %collective-permute-start.8) | collective-permute-done | bytes 98336 | tf_op jit(solution)/shard_map/ppermute | solution.py:43
  62.8 6.1 %collective-permute-done.15 = bf16[288,768]{1,0:T(8,128)(2,1)S(1)} collective-permute-done((bf16[288,768]{1,0:T(8,128)(2,1)S(1)}, bf16[288,768]{1,0:T(8,128)(2,1)S(1)}, u32[]{:S(2)}, u32[]{:S(2)}) %collective-permute-start.15) | collective-permute-done | bytes 442400 | tf_op jit(solution)/shard_map/ppermute | solution.py:43
  72.7 3.6 %collective-permute-start.19 = (bf16[40,1536]{1,0:T(8,128)(2,1)S(1)}, bf16[40,1536]{1,0:T(8,128)(2,1)S(1)}, u32[]{:S(2)}, u32[]{:S(2)}) collective-permute-start(bf16[40,1536]{1,0:T(8,128)(2,1)S(1)} %get-tuple-element.83), channel_id=1, source_target_pairs={{0,24},{4,28},{8,16},{12,20},{16,8},{20,12},{24,0},{28,4},{1,25},{... | collective-permute-start | bytes 368648 | tf_op jit(solution)/shard_map/ppermute | solution.py:43
  76.6 9.5 %collective-permute-done.17 = bf16[40,1536]{1,0:T(8,128)(2,1)S(1)} collective-permute-done((bf16[40,1536]{1,0:T(8,128)(2,1)S(1)}, bf16[40,1536]{1,0:T(8,128)(2,1)S(1)}, u32[]{:S(2)}, u32[]{:S(2)}) %collective-permute-start.17) | collective-permute-done | bytes 122912 | tf_op jit(solution)/shard_map/ppermute | solution.py:43
  86.1 3.2 %collective-permute-done.18 = bf16[40,1536]{1,0:T(8,128)(2,1)S(1)} collective-permute-done((bf16[40,1536]{1,0:T(8,128)(2,1)S(1)}, bf16[40,1536]{1,0:T(8,128)(2,1)S(1)}, u32[]{:S(2)}, u32[]{:S(2)}) %collective-permute-start.18) | collective-permute-done | bytes 122912 | tf_op jit(solution)/shard_map/ppermute | solution.py:43
  115.5 4.6 %collective-permute-start.25 = (bf16[40,1536]{1,0:T(8,128)(2,1)S(1)}, bf16[40,1536]{1,0:T(8,128)(2,1)S(1)}, u32[]{:S(2)}, u32[]{:S(2)}) collective-permute-start(bf16[40,1536]{1,0:T(8,128)(2,1)S(1)} %get-tuple-element.159), channel_id=1, source_target_pairs={{0,8},{4,12},{8,0},{12,4},{16,24},{20,28},{24,16},{28,20},{1,9},{5... | collective-permute-start | bytes 368648 | tf_op jit(solution)/shard_map/ppermute | solution.py:43
  120.8 4.0 %collective-permute-start.27 = (bf16[40,1536]{1,0:T(8,128)(2,1)S(1)}, bf16[40,1536]{1,0:T(8,128)(2,1)S(1)}, u32[]{:S(2)}, u32[]{:S(2)}) collective-permute-start(bf16[40,1536]{1,0:T(8,128)(2,1)S(1)} %get-tuple-element.157), channel_id=1, source_target_pairs={{0,16},{4,20},{8,24},{12,28},{16,0},{20,4},{24,8},{28,12},{1,17},{... | collective-permute-start | bytes 368648 | tf_op jit(solution)/shard_map/ppermute | solution.py:43
  127.6 3.6 %collective-permute-done.26 = bf16[40,1536]{1,0:T(8,128)(2,1)S(1)} collective-permute-done((bf16[40,1536]{1,0:T(8,128)(2,1)S(1)}, bf16[40,1536]{1,0:T(8,128)(2,1)S(1)}, u32[]{:S(2)}, u32[]{:S(2)}) %collective-permute-start.26) | collective-permute-done | bytes 122912 | tf_op jit(solution)/shard_map/ppermute | solution.py:43
  133.0 10.0 %collective-permute-done.28 = bf16[40,1536]{1,0:T(8,128)(2,1)S(1)} collective-permute-done((bf16[40,1536]{1,0:T(8,128)(2,1)S(1)}, bf16[40,1536]{1,0:T(8,128)(2,1)S(1)}, u32[]{:S(2)}, u32[]{:S(2)}) %collective-permute-start.28) | collective-permute-done | bytes 122912 | tf_op jit(solution)/shard_map/ppermute | solution.py:43
  150.4 3.9 %collective-permute-done.32.g2 = bf16[256,192]{1,0:T(8,128)(2,1)S(1)} collective-permute-done((bf16[256,192]{1,0:T(8,128)(2,1)S(1)}, bf16[256,192]{1,0:T(8,128)(2,1)S(1)}, u32[]{:S(2)}, u32[]{:S(2)}) %collective-permute-start.32) | collective-permute-done | bytes 98336 | tf_op jit(solution)/shard_map/ppermute | solution.py:43
  155.8 7.7 %attention_backward_0.1 = (bf16[1024,192]{1,0:T(8,128)(2,1)S(1)}, bf16[192,768]{1,0:T(8,128)(2,1)S(1)}, f32[8,768]{1,0:T(8,128)S(1)}) custom-call(s32[1]{0:T(128)} %bitcast.me_ref, f32[32,3]{1,0:T(8,128)S(1)} %copy.31.table_ref, s32[4,1,256]{2,1,0:T(1,128)S(1)} %bitcast.92, s32[4,256,1]{2,1,0:T(8,128)S(1)} %reshape.141.seg_col_ref, ...), custom_call_target="tpu_custom_call" | custom-call | flops 8000000000 | bytes 6000000 | tf_op jit(solution)/shard_map/attention_backward_0/pallas_call | solution.py:416
  167.1 8.0 %attention_backward_1.1 = (bf16[1024,192]{1,0:T(8,128)(2,1)S(1)}, bf16[192,768]{1,0:T(8,128)(2,1)S(1)}, f32[8,768]{1,0:T(8,128)S(1)}) custom-call(s32[1]{0:T(128)} %bitcast.me_ref, f32[32,3]{1,0:T(8,128)S(1)} %copy.31.table_ref, s32[4,1,256]{2,1,0:T(1,128)S(1)} %bitcast.93, s32[4,256,1]{2,1,0:T(8,128)S(1)} %reshape.141.seg_col_ref, ...), custom_call_target="tpu_custom_call" | custom-call | flops 8000000000 | bytes 6000000 | tf_op jit(solution)/shard_map/attention_backward_1/pallas_call | solution.py:416
  175.1 10.3 %attention_backward_2.1 = (bf16[1024,768]{1,0:T(8,128)(2,1)}, bf16[192,768]{1,0:T(8,128)(2,1)S(1)}, f32[8,768]{1,0:T(8,128)S(1)}) custom-call(s32[1]{0:T(128)} %bitcast.me_ref, f32[32,3]{1,0:T(8,128)S(1)} %copy.31.table_ref, s32[4,1,256]{2,1,0:T(1,128)S(1)} %bitcast.94, s32[4,256,1]{2,1,0:T(8,128)S(1)} %reshape.141.seg_col_ref, ...), custom_call_target="tpu_custom_call" | custom-call | flops 8000000000 | bytes 6000000 | tf_op jit(solution)/shard_map/attention_backward_2/pallas_call | solution.py:416
  189.0 5.2 %collective-permute-start.39 = (bf16[192,768]{1,0:T(8,128)(2,1)S(1)}, bf16[192,768]{1,0:T(8,128)(2,1)S(1)}, u32[]{:S(2)}, u32[]{:S(2)}) collective-permute-start(bf16[192,768]{1,0:T(8,128)(2,1)S(1)} %get-tuple-element.198), channel_id=1, source_target_pairs={{0,8},{4,12},{8,0},{12,4},{16,24},{20,28},{24,16},{28,20},{1,9},{5... | collective-permute-start | bytes 884744 | tf_op jit(solution)/shard_map/ppermute | solution.py:43
  196.7 4.5 %collective-permute-done.39 = bf16[192,768]{1,0:T(8,128)(2,1)S(1)} collective-permute-done((bf16[192,768]{1,0:T(8,128)(2,1)S(1)}, bf16[192,768]{1,0:T(8,128)(2,1)S(1)}, u32[]{:S(2)}, u32[]{:S(2)}) %collective-permute-start.39) | collective-permute-done | bytes 294944 | tf_op jit(solution)/shard_map/ppermute | solution.py:43
  206.7 2.8 %add_bitcast_fusion = f32[1,768,768]{2,1,0:T(8,128)} fusion(bf16[768,768]{1,0:T(8,128)(2,1)S(1)} %collective-permute-done.42, bf16[320,768]{1,0:T(8,128)(2,1)S(1)} %copy-done.29, bf16[320,768]{1,0:T(8,128)(2,1)S(1)} %copy-done.27, f32[640,768]{1,0:T(8,128)S(1)} %copy-done.68), kind=kOutput, calls=%fused_computation.5 | convolution fusion | flops 762544128 | bytes 6488064 | tf_op jit(solution)/shard_map/dot_general | solution.py:38
  209.4 3.6 %collective-permute-done.45 = f32[11,768]{1,0:T(8,128)S(1)} collective-permute-done((f32[11,768]{1,0:T(8,128)S(1)}, f32[11,768]{1,0:T(8,128)S(1)}, u32[]{:S(2)}, u32[]{:S(2)}) %collective-permute-start.45) | collective-permute-done | bytes 33824 | tf_op jit(solution)/shard_map/ppermute | solution.py:43
  214.3 2.8 %collective-permute-start.48 = (bf16[96,768]{1,0:T(8,128)(2,1)S(1)}, bf16[96,768]{1,0:T(8,128)(2,1)S(1)}, u32[]{:S(2)}, u32[]{:S(2)}) collective-permute-start(bf16[96,768]{1,0:T(8,128)(2,1)S(1)} %add_convert_fusion.5), channel_id=1, source_target_pairs={{0,16},{4,20},{8,24},{12,28},{16,0},{20,4},{24,8},{28,12},{1,17},{... | collective-permute-start | bytes 442376 | tf_op jit(solution)/shard_map/ppermute | solution.py:43
  218.6 7.9 %collective-permute-done.48 = bf16[96,768]{1,0:T(8,128)(2,1)S(1)} collective-permute-done((bf16[96,768]{1,0:T(8,128)(2,1)S(1)}, bf16[96,768]{1,0:T(8,128)(2,1)S(1)}, u32[]{:S(2)}, u32[]{:S(2)}) %collective-permute-start.48) | collective-permute-done | bytes 147488 | tf_op jit(solution)/shard_map/ppermute | solution.py:43
  232.1 3.6 %collective-permute-done.52 = f32[11,768]{1,0:T(8,128)S(1)} collective-permute-done((f32[11,768]{1,0:T(8,128)S(1)}, f32[11,768]{1,0:T(8,128)S(1)}, u32[]{:S(2)}, u32[]{:S(2)}) %collective-permute-start.52) | collective-permute-done | bytes 33824 | tf_op jit(solution)/shard_map/ppermute | solution.py:43
  237.3 2.9 %collective-permute-start.55 = (f32[11,768]{1,0:T(8,128)S(1)}, f32[11,768]{1,0:T(8,128)S(1)}, u32[]{:S(2)}, u32[]{:S(2)}) collective-permute-start(f32[11,768]{1,0:T(8,128)S(1)} %add.175), channel_id=1, source_target_pairs={{0,16},{4,20},{8,24},{12,28},{16,0},{20,4},{24,8},{28,12},{1,17},{... | collective-permute-start | bytes 101384 | tf_op jit(solution)/shard_map/ppermute | solution.py:43
  (348 shorter events, 112.9 us)
Async XLA Ops:
  4.3 16.0 %collective-permute-start = (bf16[256,768]{1,0:T(8,128)(2,1)S(1)}, bf16[256,768]{1,0:T(8,128)(2,1)S(1)}, u32[]{:S(2)}, u32[]{:S(2)}) collective-permute-start(bf16[256,768]{1,0:T(8,128)(2,1)S(1)} %fusion.33.x0), channel_id=1, source_target_pairs={{0,1},{1,0},{2,3},{3,2},{4,5},{5,4},{6,7},{7,6},{8,9},{9,8},{10,11... | collective-permute-start | bytes 1179656 | tf_op jit(solution)/shard_map/ppermute | solution.py:43
  9.2 31.1 %collective-permute-start.5 = (bf16[480,768]{1,0:T(8,128)(2,1)}, bf16[480,768]{1,0:T(8,128)(2,1)}, u32[]{:S(2)}, u32[]{:S(2)}) collective-permute-start(bf16[480,768]{1,0:T(8,128)(2,1)} %slice_bitcast_fusion.4), channel_id=1, source_target_pairs={{0,2},{1,3},{2,0},{3,1},{4,6},{5,7},{6,4},{7,5},{8,10},{9,11},{10,... | collective-permute-start | bytes 2211848 | tf_op jit(solution)/shard_map/ppermute | solution.py:43
  11.1 29.2 %collective-permute-start.10 = (bf16[192,768]{1,0:T(8,128)(2,1)}, bf16[192,768]{1,0:T(8,128)(2,1)}, u32[]{:S(2)}, u32[]{:S(2)}) collective-permute-start(bf16[192,768]{1,0:T(8,128)(2,1)} %param.16), channel_id=1, source_target_pairs={{0,1},{1,0},{2,3},{3,2},{4,5},{5,4},{6,7},{7,6},{8,9},{9,8},{10,11... | collective-permute-start | bytes 884744 | tf_op jit(solution)/shard_map/ppermute | solution.py:43
  18.3 21.9 %collective-permute-start.6 = (bf16[192,768]{1,0:T(8,128)(2,1)}, bf16[192,768]{1,0:T(8,128)(2,1)S(1)}, u32[]{:S(2)}, u32[]{:S(2)}) collective-permute-start(bf16[192,768]{1,0:T(8,128)(2,1)} %param.16), channel_id=1, source_target_pairs={{0,2},{1,3},{2,0},{3,1},{4,6},{5,7},{6,4},{7,5},{8,10},{9,11},{10,... | collective-permute-start | bytes 884744 | tf_op jit(solution)/shard_map/ppermute | solution.py:43
  43.6 15.0 %collective-permute-start.16 = (bf16[256,768]{1,0:T(8,128)(2,1)S(1)}, bf16[256,768]{1,0:T(8,128)(2,1)S(1)}, u32[]{:S(2)}, u32[]{:S(2)}) collective-permute-start(bf16[256,768]{1,0:T(8,128)(2,1)S(1)} %copy-done.34), channel_id=1, source_target_pairs={{0,2},{1,3},{2,0},{3,1},{4,6},{5,7},{6,4},{7,5},{8,10},{9,11},{10,... | collective-permute-start | bytes 1179656 | tf_op jit(solution)/shard_map/ppermute | solution.py:43
  55.8 13.0 %collective-permute-start.15 = (bf16[288,768]{1,0:T(8,128)(2,1)S(1)}, bf16[288,768]{1,0:T(8,128)(2,1)S(1)}, u32[]{:S(2)}, u32[]{:S(2)}) collective-permute-start(bf16[288,768]{1,0:T(8,128)(2,1)S(1)} %slice_bitcast_fusion.5), channel_id=1, source_target_pairs={{0,2},{1,3},{2,0},{3,1},{4,6},{5,7},{6,4},{7,5},{8,10},{9,11},{10,... | collective-permute-start | bytes 1327112 | tf_op jit(solution)/shard_map/ppermute | solution.py:43
  58.2 13.2 %collective-permute-start.14 = (bf16[40,1536]{1,0:T(8,128)(2,1)S(1)}, bf16[40,1536]{1,0:T(8,128)(2,1)S(1)}, u32[]{:S(2)}, u32[]{:S(2)}) collective-permute-start(bf16[40,1536]{1,0:T(8,128)(2,1)S(1)} %get-tuple-element.170), channel_id=1, source_target_pairs={{0,12},{4,8},{8,4},{12,0},{16,28},{20,24},{24,20},{28,16},{1,13},{... | collective-permute-start | bytes 368648 | tf_op jit(solution)/shard_map/ppermute | solution.py:43
  58.6 30.8 %collective-permute-start.21 = (bf16[512,768]{1,0:T(8,128)(2,1)S(1)}, bf16[512,768]{1,0:T(8,128)(2,1)S(1)}, u32[]{:S(2)}, u32[]{:S(2)}) collective-permute-start(bf16[512,768]{1,0:T(8,128)(2,1)S(1)} %copy-done.25), channel_id=1, source_target_pairs={{0,2},{1,3},{2,0},{3,1},{4,6},{5,7},{6,4},{7,5},{8,10},{9,11},{10,... | collective-permute-start | bytes 2359304 | tf_op jit(solution)/shard_map/ppermute | solution.py:43
  68.9 17.2 %collective-permute-start.17 = (bf16[40,1536]{1,0:T(8,128)(2,1)S(1)}, bf16[40,1536]{1,0:T(8,128)(2,1)S(1)}, u32[]{:S(2)}, u32[]{:S(2)}) collective-permute-start(bf16[40,1536]{1,0:T(8,128)(2,1)S(1)} %get-tuple-element.81), channel_id=1, source_target_pairs={{0,16},{4,20},{8,24},{12,28},{16,0},{20,4},{24,8},{28,12},{1,17},{... | collective-permute-start | bytes 368648 | tf_op jit(solution)/shard_map/ppermute | solution.py:43
  71.5 17.9 %collective-permute-start.18 = (bf16[40,1536]{1,0:T(8,128)(2,1)S(1)}, bf16[40,1536]{1,0:T(8,128)(2,1)S(1)}, u32[]{:S(2)}, u32[]{:S(2)}) collective-permute-start(bf16[40,1536]{1,0:T(8,128)(2,1)S(1)} %get-tuple-element.82), channel_id=1, source_target_pairs={{0,20},{4,16},{8,28},{12,24},{16,4},{20,0},{24,12},{28,8},{1,21},{... | collective-permute-start | bytes 368648 | tf_op jit(solution)/shard_map/ppermute | solution.py:43
  72.7 16.7 %collective-permute-start.19 = (bf16[40,1536]{1,0:T(8,128)(2,1)S(1)}, bf16[40,1536]{1,0:T(8,128)(2,1)S(1)}, u32[]{:S(2)}, u32[]{:S(2)}) collective-permute-start(bf16[40,1536]{1,0:T(8,128)(2,1)S(1)} %get-tuple-element.83), channel_id=1, source_target_pairs={{0,24},{4,28},{8,16},{12,20},{16,8},{20,12},{24,0},{28,4},{1,25},{... | collective-permute-start | bytes 368648 | tf_op jit(solution)/shard_map/ppermute | solution.py:43
  76.3 13.1 %collective-permute-start.20 = (bf16[40,1536]{1,0:T(8,128)(2,1)S(1)}, bf16[40,1536]{1,0:T(8,128)(2,1)S(1)}, u32[]{:S(2)}, u32[]{:S(2)}) collective-permute-start(bf16[40,1536]{1,0:T(8,128)(2,1)S(1)} %get-tuple-element.84), channel_id=1, source_target_pairs={{0,28},{4,24},{8,20},{12,16},{16,12},{20,8},{24,4},{28,0},{1,29},{... | collective-permute-start | bytes 368648 | tf_op jit(solution)/shard_map/ppermute | solution.py:43
  111.5 13.4 %collective-permute-start.24 = (bf16[40,1536]{1,0:T(8,128)(2,1)S(1)}, bf16[40,1536]{1,0:T(8,128)(2,1)S(1)}, u32[]{:S(2)}, u32[]{:S(2)}) collective-permute-start(bf16[40,1536]{1,0:T(8,128)(2,1)S(1)} %get-tuple-element.160), channel_id=1, source_target_pairs={{0,4},{4,0},{8,12},{12,8},{16,20},{20,16},{24,28},{28,24},{1,5},{5... | collective-permute-start | bytes 368648 | tf_op jit(solution)/shard_map/ppermute | solution.py:43
  113.9 29.2 %collective-permute-start.31 = (bf16[768,768]{1,0:T(8,128)(2,1)S(1)}, bf16[768,768]{1,0:T(8,128)(2,1)S(1)}, u32[]{:S(2)}, u32[]{:S(2)}) collective-permute-start(bf16[768,768]{1,0:T(8,128)(2,1)S(1)} %convolution_convert_fusion.2), channel_id=1, source_target_pairs={{0,2},{1,3},{2,0},{3,1},{4,6},{5,7},{6,4},{7,5},{8,10},{9,11},{10,... | collective-permute-start | bytes 3538952 | tf_op jit(solution)/shard_map/ppermute | solution.py:43
  120.8 12.2 %collective-permute-start.27 = (bf16[40,1536]{1,0:T(8,128)(2,1)S(1)}, bf16[40,1536]{1,0:T(8,128)(2,1)S(1)}, u32[]{:S(2)}, u32[]{:S(2)}) collective-permute-start(bf16[40,1536]{1,0:T(8,128)(2,1)S(1)} %get-tuple-element.157), channel_id=1, source_target_pairs={{0,16},{4,20},{8,24},{12,28},{16,0},{20,4},{24,8},{28,12},{1,17},{... | collective-permute-start | bytes 368648 | tf_op jit(solution)/shard_map/ppermute | solution.py:43
  124.8 18.1 %collective-permute-start.28 = (bf16[40,1536]{1,0:T(8,128)(2,1)S(1)}, bf16[40,1536]{1,0:T(8,128)(2,1)S(1)}, u32[]{:S(2)}, u32[]{:S(2)}) collective-permute-start(bf16[40,1536]{1,0:T(8,128)(2,1)S(1)} %get-tuple-element.156), channel_id=1, source_target_pairs={{0,20},{4,16},{8,28},{12,24},{16,4},{20,0},{24,12},{28,8},{1,21},{... | collective-permute-start | bytes 368648 | tf_op jit(solution)/shard_map/ppermute | solution.py:43
  125.1 17.9 %collective-permute-start.29 = (bf16[40,1536]{1,0:T(8,128)(2,1)S(1)}, bf16[40,1536]{1,0:T(8,128)(2,1)S(1)}, u32[]{:S(2)}, u32[]{:S(2)}) collective-permute-start(bf16[40,1536]{1,0:T(8,128)(2,1)S(1)} %get-tuple-element.155), channel_id=1, source_target_pairs={{0,24},{4,28},{8,16},{12,20},{16,8},{20,12},{24,0},{28,4},{1,25},{... | collective-permute-start | bytes 368648 | tf_op jit(solution)/shard_map/ppermute | solution.py:43
  131.1 11.9 %collective-permute-start.30 = (bf16[40,1536]{1,0:T(8,128)(2,1)S(1)}, bf16[40,1536]{1,0:T(8,128)(2,1)S(1)}, u32[]{:S(2)}, u32[]{:S(2)}) collective-permute-start(bf16[40,1536]{1,0:T(8,128)(2,1)S(1)} %get-tuple-element.154), channel_id=1, source_target_pairs={{0,28},{4,24},{8,20},{12,16},{16,12},{20,8},{24,4},{28,0},{1,29},{... | collective-permute-start | bytes 368648 | tf_op jit(solution)/shard_map/ppermute | solution.py:43
  150.4 13.1 %collective-permute-start.37 = (bf16[256,768]{1,0:T(8,128)(2,1)S(1)}, bf16[256,768]{1,0:T(8,128)(2,1)S(1)}, u32[]{:S(2)}, u32[]{:S(2)}) collective-permute-start(bf16[256,768]{1,0:T(8,128)(2,1)S(1)} %get-tuple-element.91), channel_id=1, source_target_pairs={{0,1},{1,0},{2,3},{3,2},{4,5},{5,4},{6,7},{7,6},{8,9},{9,8},{10,11... | collective-permute-start | bytes 1179656 | tf_op jit(solution)/shard_map/ppermute | solution.py:43
  166.0 22.3 %collective-permute-start.38 = (bf16[256,768]{1,0:T(8,128)(2,1)S(1)}, bf16[256,768]{1,0:T(8,128)(2,1)S(1)}, u32[]{:S(2)}, u32[]{:S(2)}) collective-permute-start(bf16[256,768]{1,0:T(8,128)(2,1)S(1)} %collective-permute-done.34), channel_id=1, source_target_pairs={{0,1},{1,0},{2,3},{3,2},{4,5},{5,4},{6,7},{7,6},{8,9},{9,8},{10,11... | collective-permute-start | bytes 1179656 | tf_op jit(solution)/shard_map/ppermute | solution.py:43
  166.1 35.1 %collective-permute-start.42 = (bf16[768,768]{1,0:T(8,128)(2,1)S(1)}, bf16[768,768]{1,0:T(8,128)(2,1)S(1)}, u32[]{:S(2)}, u32[]{:S(2)}) collective-permute-start(bf16[768,768]{1,0:T(8,128)(2,1)S(1)} %convolution_convert_fusion.1), channel_id=1, source_target_pairs={{0,2},{1,3},{2,0},{3,1},{4,6},{5,7},{6,4},{7,5},{8,10},{9,11},{10,... | collective-permute-start | bytes 3538952 | tf_op jit(solution)/shard_map/ppermute | solution.py:43
  186.9 14.4 %collective-permute-start.41 = (bf16[2,256,768]{2,1,0:T(8,128)(2,1)S(1)}, bf16[2,256,768]{2,1,0:T(8,128)(2,1)S(1)}, u32[]{:S(2)}, u32[]{:S(2)}) collective-permute-start(bf16[2,256,768]{2,1,0:T(8,128)(2,1)S(1)} %slice_bitcast_fusion.2), channel_id=1, source_target_pairs={{0,1},{1,0},{2,3},{3,2},{4,5},{5,4},{6,7},{7,6},{8,9},{9,8},{10,11... | collective-permute-start | bytes 2359304 | tf_op jit(solution)/shard_map/ppermute | solution.py:43
  189.0 12.3 %collective-permute-start.39 = (bf16[192,768]{1,0:T(8,128)(2,1)S(1)}, bf16[192,768]{1,0:T(8,128)(2,1)S(1)}, u32[]{:S(2)}, u32[]{:S(2)}) collective-permute-start(bf16[192,768]{1,0:T(8,128)(2,1)S(1)} %get-tuple-element.198), channel_id=1, source_target_pairs={{0,8},{4,12},{8,0},{12,4},{16,24},{20,28},{24,16},{28,20},{1,9},{5... | collective-permute-start | bytes 884744 | tf_op jit(solution)/shard_map/ppermute | solution.py:43
  214.3 12.1 %collective-permute-start.48 = (bf16[96,768]{1,0:T(8,128)(2,1)S(1)}, bf16[96,768]{1,0:T(8,128)(2,1)S(1)}, u32[]{:S(2)}, u32[]{:S(2)}) collective-permute-start(bf16[96,768]{1,0:T(8,128)(2,1)S(1)} %add_convert_fusion.5), channel_id=1, source_target_pairs={{0,16},{4,20},{8,24},{12,28},{16,0},{20,4},{24,8},{28,12},{1,17},{... | collective-permute-start | bytes 442376 | tf_op jit(solution)/shard_map/ppermute | solution.py:43
  (103 other events, 781.6 us)
